TPU v7x, 1024 devices: a whole 8x8x8 slice. The times are simulated.
1024 devices in a mesh: dp: 16 (over y, core), expert: 64 (over z, x).
Axes of the slice: x: 8, y: 8, z: 8, core: 2. Of those that a mesh axis runs over, the one named last changes fastest.
Arguments:
- grad_out: bfloat16 [2048, 7168], P('expert', 'dp'), may hold values from -6 to 6
- probs: float32 [2048, 2], P('expert'), may hold values from 0.25 to 1
- expert_ids: int32 [2048, 2], P('expert'), may hold values from 0 to 3, all different within a row; in each aligned block of 32 rows (0 to 31, 32 to 63, ...) at most 32 rows name the same one
- x_saved: bfloat16 [4, 2048, 7168], P(None, None, 'dp'), may hold values from -6 to 6
- gate_act: bfloat16 [2048, 19456], P(None, 'expert'), may hold values from -6 to 6
- up_act: bfloat16 [2048, 19456], P(None, 'expert'), may hold values from -6 to 6
- w_up: bfloat16 [7168, 19456], P('dp', 'expert'), may hold values from -0.0625 to 0.0625
- w_down: bfloat16 [19456, 7168], P('expert', 'dp'), may hold values from -0.078125 to 0.078125
Outputs:
- grad_tokens: bfloat16 [2048, 7168], P('expert', 'dp')
- grad_w_up: bfloat16 [7168, 19456], P('dp', 'expert')
- grad_w_down: bfloat16 [19456, 7168], P('expert', 'dp')
Inputs may be any that keep to these rules, and one draw needn't show every extreme that they name: `expert_ids`: the two experts of a token differ. Among the 32 tokens of one index of expert no expert is named more than 32 times, and in some such block one expert is named exactly 32 times.
All inputs are finite; a program needn't handle non-finite values.
Results may differ from a plain program's by a relative error of at most 0.0064.
Values may be sent and summed in bfloat16 or wider, within the bound.
A program may use at most 64 MiB of HBM per device.

v0:
```python
import jax
import jax.numpy as jnp
from jax import lax
from jax.sharding import PartitionSpec as P

CAP = 32


def body(grad_out, probs, expert_ids, x_saved, gate_act, up_act, w_up, w_down):
    experts = x_saved.shape[0]
    sources = lax.axis_size("expert")
    group_size = sources // experts
    feature_count = grad_out.shape[1]
    slot_count = CAP * sources
    position = lax.axis_index("expert")
    own_expert = position // group_size
    flat_ids = expert_ids.reshape(-1)
    onehot = (flat_ids[:, None] == jnp.arange(experts, dtype=jnp.int32)[None, :]).astype(jnp.int32)
    before = jnp.cumsum(onehot, axis=0) - onehot
    slot_rank = jnp.sum(before * onehot, axis=1)
    targets = slot_rank * experts + flat_ids
    scaled_rows = (probs[:, :, None] * grad_out[:, None, :].astype(jnp.float32)).astype(
        jnp.bfloat16
    )
    scaled_rows = scaled_rows.reshape(-1, feature_count)
    placing = (jnp.arange(CAP * experts, dtype=jnp.int32)[:, None] == targets[None, :]).astype(
        jnp.bfloat16
    )
    send_rows = jnp.dot(placing, scaled_rows, preferred_element_type=jnp.float32).astype(
        jnp.bfloat16
    )
    send_rows = send_rows.reshape(CAP, experts, feature_count)
    copies = jnp.repeat(send_rows, group_size, axis=1)
    arrived = lax.all_to_all(copies, "expert", split_axis=1, concat_axis=1, tiled=True)
    routed = arrived.reshape(slot_count, feature_count)
    partial_sum = jnp.dot(routed, w_down.T, preferred_element_type=jnp.float32)
    total_sum = lax.psum(partial_sum, "dp")
    unit_grad = (total_sum * gate_act.astype(jnp.float32)).astype(jnp.bfloat16)
    hidden = (gate_act.astype(jnp.float32) * up_act.astype(jnp.float32)).astype(jnp.bfloat16)
    grad_w_down = jnp.dot(hidden.T, routed, preferred_element_type=jnp.float32).astype(jnp.bfloat16)
    x_mine = lax.dynamic_index_in_dim(x_saved, own_expert, 0, keepdims=False)
    grad_w_up = jnp.dot(x_mine.T, unit_grad, preferred_element_type=jnp.float32).astype(
        jnp.bfloat16
    )
    slot_terms = jnp.dot(unit_grad, w_up.T, preferred_element_type=jnp.float32).astype(jnp.bfloat16)
    returned = lax.all_to_all(
        slot_terms.reshape(CAP, sources, feature_count),
        "expert",
        split_axis=1,
        concat_axis=1,
        tiled=True,
    )
    summed = jnp.sum(
        returned.reshape(CAP, experts, group_size, feature_count).astype(jnp.float32), axis=2
    )
    picked = jnp.take(summed.reshape(CAP * experts, feature_count), targets, axis=0)
    grad_tokens = jnp.sum(picked.reshape(-1, 2, feature_count), axis=1).astype(jnp.bfloat16)
    return (grad_tokens, grad_w_up, grad_w_down)


def solution(mesh):
    return jax.shard_map(
        body,
        mesh=mesh,
        in_specs=(
            P("expert", "dp"),
            P("expert", None),
            P("expert", None),
            P(None, None, "dp"),
            P(None, "expert"),
            P(None, "expert"),
            P("dp", "expert"),
            P("expert", "dp"),
        ),
        out_specs=(P("expert", "dp"), P("dp", "expert"), P("expert", "dp")),
        check_vma=False,
    )
```

profile of v0, /device:TPU:55, one launch (start us, length us, event | category | flops | bytes accessed | tf_op | source)
XLA Modules:
  0.0 311.3 jit_solution(7564359871424456095)
XLA Ops:
  7.2 0.0 copy-start
  7.2 0.0 all-reduce.2.cloned.1.call-start
  7.2 0.8 copy.41
  8.0 0.1 eq.28
  8.1 0.8 copy.44
  8.9 0.1 mul.57
  9.0 0.1 fusion.15
  9.1 0.1 reduce_window_sum.11
  9.2 0.2 select_reduce_fusion.1
  9.4 0.8 mul.59
  10.2 0.1 mul.60
  10.3 0.3 convolution_convert_fusion.1
  10.6 0.1 copy.45
  10.8 0.2 broadcast_in_dim.19
  11.0 74.1 %all_to_all.10 = bf16[32,64,448]{2,0,1:T(8,128)(2,1)S(1)} all-to-all(bf16[32,64,448]{2,0,1:T(8,128)(2,1)S(1)} %bitcast.23), channel_id=1, replica_groups=mesh['dp'=16,'expert'=64] {'expert'}, dimensions={1} | all-to-all | bytes 3670016 | tf_op jit(solution)/shard_map/all_to_all | solution.py:34
  85.2 0.0 copy-start.3
  85.2 1.2 copy.47
  86.3 0.0 copy-done.3
  86.3 2.3 fusion.21
  88.6 0.0 all-reduce.2.cloned.1.call-update
  88.7 125.8 %all-reduce.2.cloned.1.call-done = f32[2048,304]{0,1:T(8,128)} async-done(((f32[2048,304]{0,1:T(8,128)}), f32[2048,304]{0,1:T(8,128)}) %all-reduce.2.cloned.1.call-update) | async-done | bytes 2490384 | tf_op jit(solution)/shard_map/psum | solution.py:37
  214.5 0.0 copy-done
  214.5 4.4 %convolution_convert_fusion = bf16[2048,448]{0,1:T(8,128)(2,1)} fusion(bf16[448,304]{0,1:T(8,128)(2,1)S(1)} %copy-done, f32[2048,304]{0,1:T(8,128)} %all-reduce.2.cloned.1.call-done, bf16[2048,304]{0,1:T(8,128)(2,1)} %param.12), kind=kOutput, calls=%fused_computation.4 | convolution fusion | flops 560627712 | bytes 5842944 | tf_op jit(solution)/shard_map/dot_general | solution.py:45
  218.9 3.8 %copy.48 = bf16[2048,448]{1,0:T(8,128)(2,1)} copy(bf16[2048,448]{0,1:T(8,128)(2,1)} %convolution_convert_fusion) | data formatting | bytes 3670016 | tf_op jit(solution)/shard_map/convert_element_type | solution.py:45
  222.7 4.0 %copy.49 = bf16[32,64,448]{2,0,1:T(8,128)(2,1)} copy(bf16[32,64,448]{2,1,0:T(8,128)(2,1)} %bitcast.24) | data formatting | bytes 3670016 | tf_op jit(solution)/shard_map/reshape | solution.py:47
  226.8 0.0 copy-start.4
  226.8 13.8 %all-to-all-start.1 = ((bf16[32,64,448]{2,0,1:T(8,128)(2,1)}), bf16[32,64,448]{2,0,1:T(8,128)(2,1)}, u32[]{:S(2)}, u32[]{:S(2)}) async-start(bf16[32,64,448]{2,0,1:T(8,128)(2,1)} %copy.49), calls=%async_computation.1 | async-start | bytes 4194304 | tf_op jit(solution)/shard_map/all_to_all | solution.py:46
  240.6 0.1 reshape.92
  240.7 0.1 mul.56
  240.8 0.1 copy.42
  240.9 0.0 copy-done.4
  240.9 0.1 copy.43
  241.0 0.0 copy-start.1
  241.1 0.0 copy-start.2
  241.1 3.4 %fusion.7 = bf16[304,448]{1,0:T(8,128)(2,1)} fusion(bf16[2048,448]{1,0:T(8,128)(2,1)S(1)} %bitcast.22, bf16[2048,304]{0,1:T(8,128)(2,1)} %param.12, bf16[2048,304]{0,1:T(8,128)(2,1)} %param.13), kind=kOutput, calls=%fused_computation.11 | convolution fusion | flops 560468992 | bytes 4597760 | tf_op jit(solution)/shard_map/dot_general | solution.py:40
  244.4 0.0 copy-done.1
  244.4 0.0 copy-done.2
  244.4 3.1 fusion.10
  247.5 51.9 %all-to-all-done.1 = bf16[32,64,448]{2,0,1:T(8,128)(2,1)} async-done(((bf16[32,64,448]{2,0,1:T(8,128)(2,1)}), bf16[32,64,448]{2,0,1:T(8,128)(2,1)}, u32[]{:S(2)}, u32[]{:S(2)}) %all-to-all-start.1) | async-done | bytes 1835040 | tf_op jit(solution)/shard_map/all_to_all | solution.py:46
  299.4 3.4 %convert_reduce_fusion = f32[32,4,448]{2,1,0:T(4,128)S(1)} fusion(bf16[32,64,448]{2,0,1:T(8,128)(2,1)} %all-to-all-done.1), kind=kLoop, calls=%fused_computation.1 | loop fusion | flops 1777664 | bytes 2064384 | tf_op jit(solution)/shard_map/reduce_sum | solution.py:53
  302.8 0.1 reshape.91
  302.9 0.7 gather_fusion
  303.5 0.1 gather.7
  303.6 0.9 select_reduce_fusion
  (6 shorter events, 0.1 us)
Async XLA Ops:
  7.2 207.3 %copy-start = (bf16[448,304]{0,1:T(8,128)(2,1)S(1)}, bf16[448,304]{0,1:T(8,128)(2,1)}, u32[]{:S(2)}) copy-start(bf16[448,304]{0,1:T(8,128)(2,1)} %param.14) | copy-start | bytes 817156
  7.2 207.3 %all-reduce.2.cloned.1.call-start = ((), (), s32[]{:S(2)}) async-start(), calls=%async_computation.2 | async-start | bytes 4980736 | tf_op jit(solution)/shard_map/psum | solution.py:37
  85.2 1.2 copy-start.3
  226.8 14.1 %copy-start.4 = (s32[32,2]{0,1:T(2,128)S(1)}, s32[32,2]{0,1:T(2,128)}, u32[]{:S(2)}) copy-start(s32[32,2]{0,1:T(2,128)} %param.10) | copy-start | bytes 772
  226.8 72.6 %all-to-all-start.1 = ((bf16[32,64,448]{2,0,1:T(8,128)(2,1)}), bf16[32,64,448]{2,0,1:T(8,128)(2,1)}, u32[]{:S(2)}, u32[]{:S(2)}) async-start(bf16[32,64,448]{2,0,1:T(8,128)(2,1)} %copy.49), calls=%async_computation.1 | async-start | bytes 4194304 | tf_op jit(solution)/shard_map/all_to_all | solution.py:46
  241.0 3.4 %copy-start.1 = (f32[2048,304]{0,1:T(8,128)S(1)}, f32[2048,304]{0,1:T(8,128)}, u32[]{:S(2)}) copy-start(f32[2048,304]{0,1:T(8,128)} %all-reduce.2.cloned.1.call-done) | copy-start | bytes 7471108
  241.1 3.4 %copy-start.2 = (bf16[2048,304]{0,1:T(8,128)(2,1)S(1)}, bf16[2048,304]{0,1:T(8,128)(2,1)}, u32[]{:S(2)}) copy-start(bf16[2048,304]{0,1:T(8,128)(2,1)} %param.12) | copy-start | bytes 3735556
Sparse Core Ops, SparseCore 0:
  88.8 125.6 all-reduce.1
where the time goes:
time: 312 us; the launch traced here: 311 us
  waiting for transfers between devices  178 us (57%)
  blocking collectives  74.1 us (24%)
  between operations  14.2 us (5%)
  starting transfers between devices  13.8 us (4%)
  matrix products  13.5 us (4%)
  local copies, waits for them, and re-layouts  13.4 us (4%)
  other arithmetic  4.61 us (1%)
    psum x1, waiting for transfers between devices, body(): total_sum = lax.psum(partial_sum, 'dp')  126 us
    all_to_all x1, blocking collectives, body(): lax.all_to_all(copies, 'expert', split_axis=1, concat_axis=1, tiled=True)  74.1 us
    all_to_all x1, waiting for transfers between devices, body(): lax.all_to_all(slot_terms.reshape(CAP, sources, feature_count), 'expert',...  51.9 us
    all_to_all x1, starting transfers between devices, body(): lax.all_to_all(slot_terms.reshape(CAP, sources, feature_count), 'expert',...  13.8 us
  transfers between devices with their start and end apart: 2, of which 2 were waited for; matrix products, arithmetic and copies ran while one was open for 2% of the time, Pallas kernels for 0%

commit v1 on v0

v1 whole, which is shorter than its diff:
```python
import functools

import jax
import jax.numpy as jnp
from jax import lax
from jax.experimental import pallas as pl
from jax.experimental.pallas import tpu as pltpu
from jax.sharding import PartitionSpec as P

F32, BF16 = jnp.float32, jnp.bfloat16
MESH = pl.DeviceIdType.MESH
N = 8
TOK = 32
CAP = 32
EXPERTS = 4
GROUPS = 4
ROWS = 16 * TOK
SPLIT = ((0, 160), (160, 144))


def hops(right, piece):
    return N // 2 if right == (piece == 0) else N // 2 - 1


def add(a, b):
    return a.astype(F32) + b.astype(F32)


def kernel(
    g_ref, probs_ref, ids_ref, x_hbm, gate_hbm, up_hbm, wup_hbm, wdown_hbm,
    tok_out, gup_out, gdown_out,
    shard, gath, place, routed, wdown, wup, gate, up, xt, part, pair, unit, terms, tok,
    yrecv, drecv, reduced, final,
    ld_sem, s1, r1, s2, r2, cs, cr, ys, yr, us, ur, fs, fr, ds, dr, es, er,
):
    pos, dpos = lax.axis_index("expert"), lax.axis_index("dp")
    z, x = pos // N, pos % N
    y, core = dpos // 2, dpos % 2
    expert = pos // (N * N // EXPERTS)

    def on_x(d):
        return {"expert": z * N + (x + d + N) % N}

    def on_z(d):
        return {"expert": ((z + d + N) % N) * N + x}

    def on_y(d):
        return {"dp": ((y + d + N) % N) * 2 + core}

    other = {"dp": y * 2 + (1 - core)}

    def remote(src, dst, ssem, rsem, dev):
        return pltpu.make_async_remote_copy(
            src_ref=src, dst_ref=dst, send_sem=ssem, recv_sem=rsem, device_id=dev, device_id_type=MESH
        )

    loads = [
        pltpu.make_async_copy(wdown_hbm, wdown, ld_sem.at[0]),
        pltpu.make_async_copy(gate_hbm, gate, ld_sem.at[1]),
        pltpu.make_async_copy(up_hbm, up, ld_sem.at[2]),
        pltpu.make_async_copy(wup_hbm, wup, ld_sem.at[3]),
        pltpu.make_async_copy(x_hbm.at[expert], xt, ld_sem.at[4]),
    ]
    for load in loads:
        load.start()

    barrier = pltpu.get_barrier_semaphore()
    partners = [on_x(d) for d in range(1, N)] + [on_z(d) for d in range(1, N)] + [on_y(1), on_y(-1), other]
    for dev in partners:
        pl.semaphore_signal(barrier, inc=1, device_id=dev, device_id_type=MESH)

    lane32 = lax.broadcasted_iota(jnp.int32, (TOK, TOK), 1)
    row32 = lax.broadcasted_iota(jnp.int32, (TOK, TOK), 0)
    lane128 = lax.broadcasted_iota(jnp.int32, (TOK, 128), 1)
    tail = g_ref[:, 384:512].astype(F32)
    for e in range(EXPERTS):
        named = ids_ref[...] == e
        prob_row = jnp.sum(jnp.where(named, probs_ref[...], 0.0), axis=0, keepdims=True)
        used_row = jnp.sum(jnp.where(named, 1.0, 0.0), axis=0, keepdims=True)
        prob = jnp.sum(jnp.where(lane32 == row32, prob_row, 0.0), axis=1, keepdims=True)
        used = jnp.sum(jnp.where(lane32 == row32, used_row, 0.0), axis=1, keepdims=True)
        before = jnp.sum(jnp.where(lane32 < row32, used_row, 0.0), axis=1, keepdims=True)
        high = prob.astype(BF16).astype(F32)
        middle = (prob - high).astype(BF16).astype(F32)
        rank = used * (before + 1.0) - 1.0
        for i, column in enumerate((high, middle, prob - high - middle, rank)):
            tail = jnp.where(lane128 == 64 + 4 * e + i, column, tail)
    shard[:, 0:384] = g_ref[:, 0:384]
    shard[:, 384:512] = tail.astype(BF16)
    gath[z, x, 0] = shard[0:16, :]
    gath[z, x, 1] = shard[16:32, :]

    pl.semaphore_wait(barrier, len(partners))

    first = []
    for d in range(1, N):
        for h, to in ((0, on_x), (1, on_z)):
            first.append(remote(gath.at[z, x, h], gath.at[z, x, h], s1.at[h, d - 1], r1.at[h, d - 1], to(d)))
            first[-1].start()
    for copy in first:
        copy.wait_recv()
    sent = list(first)

    def block(ref, h, index, piece):
        if h == 0:
            return ref.at[index, pl.ds(4 * piece, 4), 0]
        return ref.at[pl.ds(4 * piece, 4), index, 1]

    along = (on_z, on_x)
    here = (z, x)
    inflight = {}
    for k in range(N // 2):
        for c in range(2):
            for h in range(2):
                for r in range(2):
                    sign = 1 if r else -1
                    if k >= 1 and k - 1 < hops(r, c):
                        inflight[k - 1, c, h, r].wait_recv()
                    if k < hops(r, c):
                        view = block(gath, h, (here[h] - sign * k + N) % N, c)
                        copy = remote(view, view, s2.at[k, c, h, r], r2.at[k, c, h, r], along[h](sign))
                        copy.start()
                        inflight[k, c, h, r] = copy
                        sent.append(copy)
    for c in range(2):
        for h in range(2):
            for r in range(2):
                if hops(r, c) == N // 2:
                    inflight[N // 2 - 1, c, h, r].wait_recv()

    lane_id = lax.broadcasted_iota(jnp.int32, (ROWS, ROWS), 1)
    source = lax.broadcasted_iota(jnp.int32, (ROWS, 1), 0) // TOK
    tail_lane = lax.broadcasted_iota(jnp.int32, (ROWS, 128), 1) - 64 - 4 * expert

    def to_slots(g, carry):
        rows = gath[pl.ds(2 * g, 2)].reshape(ROWS, 512)
        extra = rows[:, 384:512].astype(F32)
        weight = jnp.sum(jnp.where((tail_lane >= 0) & (tail_lane < 3), extra, 0.0), axis=1, keepdims=True)
        rank = jnp.sum(jnp.where(tail_lane == 3, extra, 0.0), axis=1, keepdims=True)
        key = rank.astype(jnp.int32) * 16 + source
        onehot = jnp.where(key == lane_id, 1.0, 0.0).astype(BF16)
        place[g] = onehot
        scaled = (rows.astype(F32) * weight).astype(BF16)
        moved = lax.dot_general(onehot, scaled, (((0,), (0,)), ((), ())), preferred_element_type=F32)
        start = pl.multiple_of(16 * g, 16)
        routed[:, pl.ds(start, 16), :] = moved[:, 0:448].astype(BF16).reshape(CAP, 16, 448)
        return carry

    lax.fori_loop(0, GROUPS, to_slots, 0)

    loads[0].wait()

    def partial(b, carry):
        rows = routed[pl.ds(2 * b, 2)].reshape(128, 448)
        part[b] = lax.dot_general(
            wdown[...], rows, (((1,), (1,)), ((), ())), preferred_element_type=F32
        ).astype(BF16)
        return carry

    cross = []
    for i in range(N):
        lax.fori_loop((1 - core) * N + i, (1 - core) * N + i + 1, partial, 0)
        copy = remote(part.at[(1 - core) * N + i], pair.at[i], cs.at[i], cr.at[i], other)
        copy.start()
        cross.append(copy)
        sent.append(copy)
    lax.fori_loop(core * N, core * N + N, partial, 0)
    for i in range(N):
        cross[i].wait_recv()
        pair[i] = add(pair[i], part[core * N + i]).astype(BF16)

    inflight = {}
    for k in range(N // 2):
        for c, (low, size) in enumerate(SPLIT):
            for r in range(2):
                sign, far = (1 if r else -1), hops(r, c)
                target = (y + sign * (far - k) + N) % N
                view = pair.at[target, pl.ds(low, size)]
                if k >= 1 and k < far:
                    inflight[k - 1, c, r].wait_recv()
                    view[...] = add(view[...], yrecv[k - 1, c, r, 0:size]).astype(BF16)
                if k < far:
                    copy = remote(
                        view, yrecv.at[k, c, r, pl.ds(0, size)], ys.at[k, c, r], yr.at[k, c, r], on_y(sign)
                    )
                    copy.start()
                    inflight[k, c, r] = copy
                    sent.append(copy)
    for load in loads[1:]:
        load.wait()
    mine = core * N + y
    lanes = pl.ds(pl.multiple_of(mine * 128, 128), 128)
    for c, (low, size) in enumerate(SPLIT):
        total = pair[y, low:low + size].astype(F32)
        for r in range(2):
            inflight[hops(r, c) - 1, c, r].wait_recv()
            total = total + yrecv[hops(r, c) - 1, c, r, 0:size].astype(F32)
        unit[mine, low:low + size] = (total * gate[low:low + size, lanes].astype(F32)).astype(BF16)

    inflight = {}
    across = []

    def cross_piece(index, c, slot):
        view = unit.at[core * N + index, pl.ds(SPLIT[c][0], SPLIT[c][1])]
        copy = remote(view, view, fs.at[slot, c], fr.at[slot, c], other)
        copy.start()
        across.append(copy)
        sent.append(copy)

    for k in range(N // 2 + 1):
        for c, (low, size) in enumerate(SPLIT):
            for r in range(2):
                sign, far = (1 if r else -1), hops(r, c)
                index = (y - sign * k + N) % N
                if k >= 1 and k <= far:
                    inflight[k - 1, c, r].wait_recv()
                if k < far:
                    view = unit.at[core * N + index, pl.ds(low, size)]
                    copy = remote(view, view, us.at[k, c, r], ur.at[k, c, r], on_y(sign))
                    copy.start()
                    inflight[k, c, r] = copy
                    sent.append(copy)
                if (k == 0 and r == 0) or (1 <= k <= far):
                    cross_piece(index, c, (sign * k + N) % N)

    def down_block(b, carry):
        span = pl.ds(pl.multiple_of(b * 512, 512), 512)
        hidden = (gate[:, span].astype(F32) * up[:, span].astype(F32)).astype(BF16)
        rows = routed[pl.ds(8 * b, 8)].reshape(512, 448)
        return carry + jnp.dot(hidden, rows, preferred_element_type=F32)

    gdown_out[...] = lax.fori_loop(0, 4, down_block, jnp.zeros((304, 448), F32)).astype(BF16)
    for copy in across:
        copy.wait_recv()

    def slot_block(b, carry):
        rows = lax.dot_general(unit[b], wup[...], (((0,), (0,)), ((), ())), preferred_element_type=F32)
        terms[pl.ds(2 * b, 2)] = rows.astype(BF16).reshape(2, 64, 448)
        return carry

    lax.fori_loop(0, 2 * N, slot_block, 0)

    def to_tokens(g, carry):
        start = pl.multiple_of(16 * g, 16)
        rows = terms[:, pl.ds(start, 16), :].reshape(ROWS, 448)
        back = jnp.dot(place[g], rows, preferred_element_type=F32).astype(BF16)
        tok[pl.ds(2 * g, 2)] = back.reshape(2, N, 2, 16, 448)
        return carry

    lax.fori_loop(0, GROUPS, to_tokens, 0)

    inflight = {}
    for k in range(N // 2):
        for c in range(2):
            for h in range(2):
                for r in range(2):
                    sign, far = (1 if r else -1), hops(r, c)
                    view = block(tok, h, (here[h] + sign * (far - k) + N) % N, c)
                    if k >= 1 and k < far:
                        inflight[k - 1, c, h, r].wait_recv()
                        view[...] = add(view[...], drecv[k - 1, c, h, r]).astype(BF16)
                    if k < far:
                        copy = remote(view, drecv.at[k, c, h, r], ds.at[k, c, h, r], dr.at[k, c, h, r], along[h](sign))
                        copy.start()
                        inflight[k, c, h, r] = copy
                        sent.append(copy)

    def up_block(b, carry):
        span = pl.ds(pl.multiple_of(b * 128, 128), 128)
        return carry + lax.dot_general(unit[b], xt[:, span], (((1,), (1,)), ((), ())), preferred_element_type=F32)

    gup_out[...] = lax.fori_loop(0, 2 * N, up_block, jnp.zeros((304, 448), F32)).astype(BF16)

    for h in range(2):
        for c in range(2):
            total = block(tok, h, here[h], c)[...].astype(F32)
            for r in range(2):
                inflight[hops(r, c) - 1, c, h, r].wait_recv()
                total = total + drecv[hops(r, c) - 1, c, h, r].astype(F32)
            reduced[h, 4 * c:4 * c + 4] = total.astype(BF16)
    last = []
    for d in range(1, N):
        for h, to in ((0, on_x), (1, on_z)):
            away = (here[1 - h] + d) % N
            copy = remote(reduced.at[h, away], final.at[h, d - 1], es.at[h, d - 1], er.at[h, d - 1], to(d))
            copy.start()
            last.append(copy)
            sent.append(copy)
    for copy in last:
        copy.wait_recv()
    for h in range(2):
        total = reduced[h, here[1 - h]].astype(F32)
        for d in range(1, N):
            total = total + final[h, d - 1].astype(F32)
        tok_out[16 * h:16 * h + 16, :] = total.astype(BF16)
    for copy in sent:
        copy.wait_send()


def body(grad_out, probs, expert_ids, x_saved, gate_act, up_act, w_up, w_down):
    vmem, hbm = pl.BlockSpec(memory_space=pltpu.VMEM), pl.BlockSpec(memory_space=pl.ANY)
    dma = pltpu.SemaphoreType.DMA
    units, width, slots = 304, 448, 2048
    outs = pl.pallas_call(
        kernel,
        out_shape=(
            jax.ShapeDtypeStruct((TOK, width), BF16),
            jax.ShapeDtypeStruct((units, width), BF16),
            jax.ShapeDtypeStruct((units, width), BF16),
        ),
        in_specs=[vmem, vmem, vmem, hbm, hbm, hbm, hbm, hbm],
        out_specs=(vmem, vmem, vmem),
        scratch_shapes=[
            pltpu.VMEM((TOK, 512), BF16),
            pltpu.VMEM((N, N, 2, 16, 512), BF16),
            pltpu.VMEM((GROUPS, ROWS, ROWS), BF16),
            pltpu.VMEM((CAP, N * N, width), BF16),
            pltpu.VMEM((units, width), BF16),
            pltpu.VMEM((units, width), BF16),
            pltpu.VMEM((units, slots), BF16),
            pltpu.VMEM((units, slots), BF16),
            pltpu.VMEM((width, slots), BF16),
            pltpu.VMEM((2 * N, units, 128), BF16),
            pltpu.VMEM((N, units, 128), BF16),
            pltpu.VMEM((2 * N, units, 128), BF16),
            pltpu.VMEM((CAP, N * N, width), BF16),
            pltpu.VMEM((N, N, 2, 16, width), BF16),
            pltpu.VMEM((4, 2, 2, 160, 128), BF16),
            pltpu.VMEM((4, 2, 2, 2, 4, 16, width), BF16),
            pltpu.VMEM((2, N, 16, width), BF16),
            pltpu.VMEM((2, N - 1, 16, width), BF16),
            dma((5,)),
            dma((2, N - 1)), dma((2, N - 1)),
            dma((4, 2, 2, 2)), dma((4, 2, 2, 2)),
            dma((N,)), dma((N,)),
            dma((4, 2, 2)), dma((4, 2, 2)),
            dma((4, 2, 2)), dma((4, 2, 2)),
            dma((N, 2)), dma((N, 2)),
            dma((4, 2, 2, 2)), dma((4, 2, 2, 2)),
            dma((2, N - 1)), dma((2, N - 1)),
        ],
        compiler_params=pltpu.CompilerParams(
            collective_id=0, has_side_effects=True, vmem_limit_bytes=48 * 1024 * 1024
        ),
        cost_estimate=pl.CostEstimate(flops=4_000_000_000, bytes_accessed=8_000_000, transcendentals=0),
    )(
        jnp.pad(grad_out, ((0, 0), (0, 64))),
        probs.T,
        expert_ids.T,
        jnp.swapaxes(x_saved, 1, 2),
        gate_act.T,
        up_act.T,
        w_up.T,
        w_down,
    )
    return outs[0], outs[1].T, outs[2]


def solution(mesh):
    return jax.shard_map(
        body,
        mesh=mesh,
        in_specs=(
            P("expert", "dp"),
            P("expert", None),
            P("expert", None),
            P(None, None, "dp"),
            P(None, "expert"),
            P(None, "expert"),
            P("dp", "expert"),
            P("expert", "dp"),
        ),
        out_specs=(P("expert", "dp"), P("dp", "expert"), P("expert", "dp")),
        check_vma=False,
    )
```

time: 312 us -> 125 us (0.40)
  the two profiles are of different devices: /device:TPU:55 before, /device:TPU:2 now
where the time goes in v1:
time: 125 us
  Pallas kernels  115 us (92%)
  local copies, waits for them, and re-layouts  8.7 us (7%)
    pallas_call x1, Pallas kernels, body(): pl.pallas_call(kernel, out_shape=(jax.ShapeDtypeStruct((TOK, width), BF16...  115 us
    unnamed x15, local copies, waits for them, and re-layouts  7.93 us

profile of v1, /device:TPU:2, one launch (start us, length us, event | category | flops | bytes accessed | tf_op | source)
XLA Modules:
  0.0 124.8 jit_solution(8852853285042087399)
XLA Ops:
  0.6 0.8 pad.4.g_ref
  1.4 0.0 copy-start
  1.4 1.3 %copy-done = bf16[2048,304]{0,1:T(8,128)(2,1)S(1)} copy-done((bf16[2048,304]{0,1:T(8,128)(2,1)S(1)}, bf16[2048,304]{0,1:T(8,128)(2,1)}, u32[]{:S(2)}) %copy-start) | copy-done | bytes 1245208
  2.7 0.0 copy-start.1
  2.7 1.3 %copy-done.1 = bf16[2048,304]{0,1:T(8,128)(2,1)S(1)} copy-done((bf16[2048,304]{0,1:T(8,128)(2,1)S(1)}, bf16[2048,304]{0,1:T(8,128)(2,1)}, u32[]{:S(2)}) %copy-start.1) | copy-done | bytes 1245208
  4.0 0.0 copy-start.2
  4.0 1.0 copy-done.2
  5.0 0.0 copy-start.3
  5.0 1.0 copy-done.3
  5.9 0.0 copy-start.4
  5.9 0.7 copy-done.4
  6.6 0.0 copy-start.5
  6.6 0.7 copy-done.5
  7.3 115.5 %shard_map.103 = (bf16[32,448]{1,0:T(8,128)(2,1)S(1)}, bf16[304,448]{1,0:T(8,128)(2,1)S(1)}, bf16[304,448]{1,0:T(8,128)(2,1)S(1)}) custom-call(bf16[32,512]{1,0:T(8,128)(2,1)S(1)} %pad.4.g_ref, f32[2,32]{1,0:T(2,128)S(1)} %bitcast.11, s32[2,32]{1,0:T(2,128)S(1)} %bitcast.12, bf16[4,448,2048]{2,1,0:T(8,128)(2,1)} %bitcast.13, bf16[304,2048]{1,0:T(8,128)(2,1)S(1)} %bitcast.8, ...), custom_call_target="tpu_custom_call" | custom-call | flops 4000000000 | bytes 8000000 | tf_op jit(solution)/shard_map/pallas_call | solution.py:304
  122.7 0.6 copy.14
  123.4 0.7 copy.15
  124.1 0.7 copy.16
Async XLA Ops:
  1.4 1.3 %copy-start = (bf16[2048,304]{0,1:T(8,128)(2,1)S(1)}, bf16[2048,304]{0,1:T(8,128)(2,1)}, u32[]{:S(2)}) copy-start(bf16[2048,304]{0,1:T(8,128)(2,1)} %param.12) | copy-start | bytes 3735556
  2.7 1.3 %copy-start.1 = (bf16[2048,304]{0,1:T(8,128)(2,1)S(1)}, bf16[2048,304]{0,1:T(8,128)(2,1)}, u32[]{:S(2)}) copy-start(bf16[2048,304]{0,1:T(8,128)(2,1)} %param.13) | copy-start | bytes 3735556
  4.0 1.0 copy-start.2
  5.0 1.0 copy-start.3
  5.9 0.7 copy-start.4
  6.6 0.7 copy-start.5

commit v2 on v1

v2 whole, which is shorter than its diff:
```python
import functools

import jax
import jax.numpy as jnp
from jax import lax
from jax.experimental import pallas as pl
from jax.experimental.pallas import tpu as pltpu
from jax.sharding import PartitionSpec as P

F32, BF16 = jnp.float32, jnp.bfloat16
MESH = pl.DeviceIdType.MESH
N = 8
TOK = 32
CAP = 32
EXPERTS = 4
GROUPS = 4
ROWS = 16 * TOK
SPLIT = ((0, 80), (80, 80), (160, 80), (240, 64))
HALVES = ((0, 160), (160, 144))
PIECES = 4


def hops(right, piece):
    return N // 2 if right == (piece < 2) else N // 2 - 1


def add(a, b):
    return a.astype(F32) + b.astype(F32)


def kernel(
    g_hbm, probs_hbm, ids_hbm, x_hbm, gate_hbm, up_hbm, wup_hbm, wdown_hbm,
    tok_out, gup_out, gdown_out,
    g_ref, probs_ref, ids_ref, shard, gath, place, routed, routed2, wdown, wdown2, wup, gate, up, xt, pair, unit, terms,
    tok, yrecv, drecv, reduced, final, down_sum,
    ld_sem, s1, r1, s2, r2, ws, wr, cs, cr, ys, yr, us, ur, fs, fr, ds, dr, es, er,
):
    pos, dpos = lax.axis_index("expert"), lax.axis_index("dp")
    z, x = pos // N, pos % N
    y, core = dpos // 2, dpos % 2
    expert = pos // (N * N // EXPERTS)

    def on_x(d):
        return {"expert": z * N + (x + d + N) % N}

    def on_z(d):
        return {"expert": ((z + d + N) % N) * N + x}

    def on_y(d):
        return {"dp": ((y + d + N) % N) * 2 + core}

    other = {"dp": y * 2 + (1 - core)}
    along = (on_z, on_x)
    here = (z, x)
    sent = []

    def remote(src, dst, ssem, rsem, dev):
        copy = pltpu.make_async_remote_copy(
            src_ref=src, dst_ref=dst, send_sem=ssem, recv_sem=rsem, device_id=dev, device_id_type=MESH
        )
        copy.start()
        sent.append(copy)
        return copy

    loads = [
        pltpu.make_async_copy(g_hbm, g_ref, ld_sem.at[0]),
        pltpu.make_async_copy(probs_hbm, probs_ref, ld_sem.at[1]),
        pltpu.make_async_copy(ids_hbm, ids_ref, ld_sem.at[2]),
        pltpu.make_async_copy(wdown_hbm, wdown, ld_sem.at[3]),
        pltpu.make_async_copy(gate_hbm, gate, ld_sem.at[4]),
        pltpu.make_async_copy(up_hbm, up, ld_sem.at[5]),
        pltpu.make_async_copy(wup_hbm, wup, ld_sem.at[6]),
        pltpu.make_async_copy(x_hbm.at[expert], xt, ld_sem.at[7]),
    ]
    for load in loads:
        load.start()

    barrier = pltpu.get_barrier_semaphore()
    partners = [on_x(d) for d in range(1, N)] + [on_z(d) for d in range(1, N)] + [on_y(1), on_y(-1), other]
    for dev in partners:
        pl.semaphore_signal(barrier, inc=1, device_id=dev, device_id_type=MESH)

    for load in loads[0:3]:
        load.wait()
    lane32 = lax.broadcasted_iota(jnp.int32, (TOK, TOK), 1)
    row32 = lax.broadcasted_iota(jnp.int32, (TOK, TOK), 0)
    lane128 = lax.broadcasted_iota(jnp.int32, (TOK, 128), 1)
    shard[:, 384:512] = jnp.zeros((TOK, 128), BF16)
    shard[:, 0:448] = g_ref[...]
    tail = shard[:, 384:512].astype(F32)
    for e in range(EXPERTS):
        named = ids_ref[...] == e
        prob_row = jnp.sum(jnp.where(named, probs_ref[...], 0.0), axis=0, keepdims=True)
        used_row = jnp.sum(jnp.where(named, 1.0, 0.0), axis=0, keepdims=True)
        prob = jnp.sum(jnp.where(lane32 == row32, prob_row, 0.0), axis=1, keepdims=True)
        used = jnp.sum(jnp.where(lane32 == row32, used_row, 0.0), axis=1, keepdims=True)
        before = jnp.sum(jnp.where(lane32 < row32, used_row, 0.0), axis=1, keepdims=True)
        high = prob.astype(BF16).astype(F32)
        middle = (prob - high).astype(BF16).astype(F32)
        rank = used * (before + 1.0) - 1.0
        for i, column in enumerate((high, middle, prob - high - middle, rank)):
            tail = jnp.where(lane128 == 64 + 4 * e + i, column, tail)
    shard[:, 384:512] = tail.astype(BF16)
    for h in range(2):
        gath[h, here[h], 0] = shard[16 * h:16 * h + 16, :]
    loads[3].wait()

    pl.semaphore_wait(barrier, len(partners))

    first = {}
    for d in (1, 7, 2, 6, 3, 5, 4):
        for h in range(2):
            first[h, N - d] = remote(
                gath.at[h, here[h], 0], gath.at[h, here[h], N - d], s1.at[h, d - 1], r1.at[h, N - d - 1], along[1 - h](d)
            )
    down_swap = remote(wdown, wdown2, ws.at[0], wr.at[0], other)

    def piece(ref, h, index, c):
        return ref.at[h, index, pl.ds(2 * c, 2)]

    inflight = {}
    for k in range(N // 2 + 1):
        for c in (0, 3, 1, 2):
            for h in range(2):
                if k == 0:
                    for j in (2 * c, 2 * c + 1):
                        if j > 0:
                            first[h, j].wait_recv()
                for r in range(2):
                    sign, far = (1 if r else -1), hops(r, c)
                    if 1 <= k <= far:
                        inflight[k - 1, c, h, r].wait_recv()
                    if k < far:
                        view = piece(gath, h, (here[h] - sign * k + N) % N, c)
                        inflight[k, c, h, r] = remote(
                            view, view, s2.at[k, c, h, r], r2.at[k, c, h, r], along[h](sign)
                        )

    lane_id = lax.broadcasted_iota(jnp.int32, (ROWS, ROWS), 1)
    row_id = lax.broadcasted_iota(jnp.int32, (ROWS, 1), 0)
    tile = (row_id % 256) // 16
    source = jnp.where(
        row_id < 256, (tile // 8) * 8 + (tile % 8 + x) % 8, (tile // 8) * 8 + tile % 8
    )
    tail_lane = lax.broadcasted_iota(jnp.int32, (ROWS, 128), 1) - 64 - 4 * expert

    def swap(g):
        span = pl.ds(pl.multiple_of(16 * g, 16), 16)
        return pltpu.make_async_remote_copy(
            src_ref=routed.at[pl.ds((1 - core) * 16, 16), span], dst_ref=routed2.at[:, span],
            send_sem=cs.at[g], recv_sem=cr.at[g], device_id=other, device_id_type=MESH,
        )

    def to_slots(g, carry):
        one = gath[0, pl.ds(2 * g, 2)].reshape(256, 512)
        two = gath[1, :, (2 * g - z + N) % N].reshape(128, 512)
        three = gath[1, :, (2 * g + 1 - z + N) % N].reshape(128, 512)
        rows = jnp.concatenate([one, two, three], axis=0)
        extra = rows[:, 384:512].astype(F32)
        weight = jnp.sum(jnp.where((tail_lane >= 0) & (tail_lane < 3), extra, 0.0), axis=1, keepdims=True)
        rank = jnp.sum(jnp.where(tail_lane == 3, extra, 0.0), axis=1, keepdims=True)
        key = rank.astype(jnp.int32) * 16 + source
        onehot = jnp.where(key == lane_id, 1.0, 0.0).astype(BF16)
        place[g] = onehot
        scaled = (rows.astype(F32) * weight).astype(BF16)
        moved = lax.dot_general(onehot, scaled, (((0,), (0,)), ((), ())), preferred_element_type=F32)
        start = pl.multiple_of(16 * g, 16)
        routed[:, pl.ds(start, 16), :] = moved[:, 0:448].astype(BF16).reshape(CAP, 16, 448)
        swap(g).start()
        return carry

    lax.fori_loop(0, GROUPS, to_slots, 0)

    down_swap.wait_recv()
    for g in range(GROUPS):
        swap(g).wait_recv()

    def partial(i):
        mine = routed[pl.ds(core * 16 + 2 * i, 2)].reshape(128, 448)
        theirs = routed2[pl.ds(2 * i, 2)].reshape(128, 448)
        dims = (((1,), (1,)), ((), ()))
        pair[i] = (
            lax.dot_general(wdown[...], mine, dims, preferred_element_type=F32)
            + lax.dot_general(wdown2[...], theirs, dims, preferred_element_type=F32)
        ).astype(BF16)

    def down_block(b):
        span = pl.ds(512 * b, 512)
        hidden = (gate[:, span].astype(F32) * up[:, span].astype(F32)).astype(BF16)
        rows = routed[8 * b:8 * b + 8].reshape(512, 448)
        product = jnp.dot(hidden, rows, preferred_element_type=F32)
        if b == 0:
            down_sum[...] = product
        elif b < 3:
            down_sum[...] += product
        else:
            gdown_out[...] = (down_sum[...] + product).astype(BF16)

    inflight = {}
    for far in (4, 3):
        for offset in ((4,) if far == 4 else (3, -3)):
            partial((y + offset + N) % N)
        for c, (low, size) in enumerate(SPLIT):
            for r in range(2):
                if hops(r, c) == far:
                    view = pair.at[(y + (far if r else -far) + N) % N, pl.ds(low, size)]
                    inflight[0, c, r] = remote(
                        view, yrecv.at[0, c, r, pl.ds(0, size)], ys.at[0, c, r], yr.at[0, c, r], on_y(1 if r else -1)
                    )
    for offset in (2, -2, 1, -1, 0):
        partial((y + offset + N) % N)
    for k in range(1, N // 2):
        for c, (low, size) in enumerate(SPLIT):
            for r in range(2):
                sign, far = (1 if r else -1), hops(r, c)
                if k < far:
                    view = pair.at[(y + sign * (far - k) + N) % N, pl.ds(low, size)]
                    inflight[k - 1, c, r].wait_recv()
                    view[...] = add(view[...], yrecv[k - 1, c, r, 0:size]).astype(BF16)
                    inflight[k, c, r] = remote(
                        view, yrecv.at[k, c, r, pl.ds(0, size)], ys.at[k, c, r], yr.at[k, c, r], on_y(sign)
                    )
        if k == 1:
            for load in loads[4:6]:
                load.wait()
        down_block(k - 1)
    for load in loads[6:]:
        load.wait()

    mine = core * N + y
    lanes = pl.ds(pl.multiple_of(mine * 128, 128), 128)
    gathering = {}
    for c, (low, size) in enumerate(SPLIT):
        total = pair[y, low:low + size].astype(F32)
        for r in range(2):
            inflight[hops(r, c) - 1, c, r].wait_recv()
            total = total + yrecv[hops(r, c) - 1, c, r, 0:size].astype(F32)
        unit[mine, low:low + size] = (total * gate[low:low + size, lanes].astype(F32)).astype(BF16)
        view = unit.at[mine, pl.ds(low, size)]
        for r in range(2):
            gathering[0, c, r] = remote(view, view, us.at[0, c, r], ur.at[0, c, r], on_y(1 if r else -1))
    across = {}

    def cross_half(k, h, r, index):
        view = unit.at[core * N + index, pl.ds(HALVES[h][0], HALVES[h][1])]
        across[k, h, r] = remote(view, view, fs.at[k, h, r], fr.at[k, h, r], other)

    def slot_block(b):
        rows = lax.dot_general(unit[b], wup[...], (((0,), (0,)), ((), ())), preferred_element_type=F32)
        terms[pl.ds(2 * b, 2)] = rows.astype(BF16).reshape(2, 64, 448)

    for h in range(2):
        cross_half(0, h, 1, y)
    down_block(3)
    slot_block(mine)

    def theirs(k):
        for h in range(2):
            for r in range(2):
                if (k, h, r) in across:
                    across[k, h, r].wait_recv()
        slot_block((1 - core) * N + (y + k) % N)
        if 0 < k < N // 2:
            slot_block((1 - core) * N + (y - k + N) % N)

    for k in range(1, N // 2 + 1):
        for c, (low, size) in enumerate(SPLIT):
            for r in range(2):
                sign, far = (1 if r else -1), hops(r, c)
                index = (y - sign * k + N) % N
                if k <= far:
                    gathering[k - 1, c, r].wait_recv()
                if k < far:
                    view = unit.at[core * N + index, pl.ds(low, size)]
                    gathering[k, c, r] = remote(view, view, us.at[k, c, r], ur.at[k, c, r], on_y(sign))
                if k <= far and c % 2 == 1:
                    cross_half(k, c // 2, r, index)
        slot_block(core * N + (y + k) % N)
        if k < N // 2:
            slot_block(core * N + (y - k + N) % N)
        theirs(k - 1)
    theirs(N // 2)

    def to_tokens(g, carry):
        start = pl.multiple_of(16 * g, 16)
        rows = terms[:, pl.ds(start, 16), :].reshape(ROWS, 448)
        back = jnp.dot(place[g], rows, preferred_element_type=F32).astype(BF16)
        tok[0, pl.ds(2 * g, 2)] = back[0:256].reshape(2, N, 16, 448)
        tok[1, :, (2 * g - z + N) % N] = back[256:384].reshape(N, 16, 448)
        tok[1, :, (2 * g + 1 - z + N) % N] = back[384:512].reshape(N, 16, 448)
        return carry

    lax.fori_loop(0, GROUPS, to_tokens, 0)

    inflight = {}
    for k in range(N // 2):
        for c in range(PIECES):
            for h in range(2):
                for r in range(2):
                    sign, far = (1 if r else -1), hops(r, c)
                    view = piece(tok, h, (here[h] + sign * (far - k) + N) % N, c)
                    if 1 <= k < far:
                        inflight[k - 1, c, h, r].wait_recv()
                        view[...] = add(view[...], drecv[k - 1, c, h, r]).astype(BF16)
                    if k < far:
                        inflight[k, c, h, r] = remote(
                            view, drecv.at[k, c, h, r], ds.at[k, c, h, r], dr.at[k, c, h, r], along[h](sign)
                        )

    def up_block(b, carry):
        span = pl.ds(pl.multiple_of(b * 128, 128), 128)
        return carry + lax.dot_general(unit[b], xt[:, span], (((1,), (1,)), ((), ())), preferred_element_type=F32)

    gup_out[...] = lax.fori_loop(0, 2 * N, up_block, jnp.zeros((304, 448), F32)).astype(BF16)

    last = []
    for c in range(PIECES):
        for h in range(2):
            total = piece(tok, h, here[h], c)[...].astype(F32)
            for r in range(2):
                inflight[hops(r, c) - 1, c, h, r].wait_recv()
                total = total + drecv[hops(r, c) - 1, c, h, r].astype(F32)
            reduced[h, 2 * c:2 * c + 2] = total.astype(BF16)
            for d in (2 * c, 2 * c + 1):
                if d > 0:
                    last.append(
                        remote(reduced.at[h, d], final.at[h, d - 1], es.at[h, d - 1], er.at[h, d - 1], along[1 - h](d))
                    )
    for copy in last:
        copy.wait_recv()
    for h in range(2):
        total = reduced[h, 0].astype(F32)
        for d in range(1, N):
            total = total + final[h, d - 1].astype(F32)
        tok_out[16 * h:16 * h + 16, :] = total.astype(BF16)
    for copy in sent:
        copy.wait_send()
    for g in range(GROUPS):
        swap(g).wait_send()


def body(grad_out, probs, expert_ids, x_saved, gate_act, up_act, w_up, w_down):
    vmem, hbm = pl.BlockSpec(memory_space=pltpu.VMEM), pl.BlockSpec(memory_space=pl.ANY)
    dma = pltpu.SemaphoreType.DMA
    units, width, slots = 304, 448, 2048
    outs = pl.pallas_call(
        kernel,
        out_shape=(
            jax.ShapeDtypeStruct((TOK, width), BF16),
            jax.ShapeDtypeStruct((units, width), BF16),
            jax.ShapeDtypeStruct((units, width), BF16),
        ),
        in_specs=[hbm] * 8,
        out_specs=(vmem, vmem, vmem),
        scratch_shapes=[
            pltpu.VMEM((TOK, width), BF16),
            pltpu.VMEM((2, TOK), F32),
            pltpu.VMEM((2, TOK), jnp.int32),
            pltpu.VMEM((TOK, 512), BF16),
            pltpu.VMEM((2, N, N, 16, 512), BF16),
            pltpu.VMEM((GROUPS, ROWS, ROWS), BF16),
            pltpu.VMEM((CAP, N * N, width), BF16),
            pltpu.VMEM((CAP // 2, N * N, width), BF16),
            pltpu.VMEM((units, width), BF16),
            pltpu.VMEM((units, width), BF16),
            pltpu.VMEM((units, width), BF16),
            pltpu.VMEM((units, slots), BF16),
            pltpu.VMEM((units, slots), BF16),
            pltpu.VMEM((width, slots), BF16),
            pltpu.VMEM((N, units, 128), BF16),
            pltpu.VMEM((2 * N, units, 128), BF16),
            pltpu.VMEM((CAP, N * N, width), BF16),
            pltpu.VMEM((2, N, N, 16, width), BF16),
            pltpu.VMEM((4, PIECES, 2, 80, 128), BF16),
            pltpu.VMEM((4, PIECES, 2, 2, 2, 16, width), BF16),
            pltpu.VMEM((2, N, 16, width), BF16),
            pltpu.VMEM((2, N - 1, 16, width), BF16),
            pltpu.VMEM((units, width), F32),
            dma((8,)),
            dma((2, N - 1)), dma((2, N - 1)),
            dma((4, PIECES, 2, 2)), dma((4, PIECES, 2, 2)),
            dma((1,)), dma((1,)),
            dma((GROUPS,)), dma((GROUPS,)),
            dma((4, PIECES, 2)), dma((4, PIECES, 2)),
            dma((4, PIECES, 2)), dma((4, PIECES, 2)),
            dma((5, 2, 2)), dma((5, 2, 2)),
            dma((4, PIECES, 2, 2)), dma((4, PIECES, 2, 2)),
            dma((2, N - 1)), dma((2, N - 1)),
        ],
        compiler_params=pltpu.CompilerParams(
            collective_id=0, has_side_effects=True, vmem_limit_bytes=60 * 1024 * 1024
        ),
        cost_estimate=pl.CostEstimate(flops=4_000_000_000, bytes_accessed=8_000_000, transcendentals=0),
    )(
        grad_out,
        probs.T,
        expert_ids.T,
        jnp.swapaxes(x_saved, 1, 2),
        gate_act.T,
        up_act.T,
        w_up.T,
        w_down,
    )
    return outs[0], outs[1].T, outs[2]


def solution(mesh):
    return jax.shard_map(
        body,
        mesh=mesh,
        in_specs=(
            P("expert", "dp"),
            P("expert", None),
            P("expert", None),
            P(None, None, "dp"),
            P(None, "expert"),
            P(None, "expert"),
            P("dp", "expert"),
            P("expert", "dp"),
        ),
        out_specs=(P("expert", "dp"), P("dp", "expert"), P("expert", "dp")),
        check_vma=False,
    )
```

time: 125 us -> 110 us (0.88)
  the two profiles are of different devices: /device:TPU:2 before, /device:TPU:16 now
where the time goes in v2:
time: 110 us; the launch traced here: 109 us
  Pallas kernels  104 us (95%)
  local copies, waits for them, and re-layouts  4.79 us (4%)
    pallas_call x1, Pallas kernels, body(): pl.pallas_call(kernel, out_shape=(jax.ShapeDtypeStruct((TOK, width), BF16...  104 us
    unnamed x3, local copies, waits for them, and re-layouts  4.79 us

profile of v2, /device:TPU:16, one launch (start us, length us, event | category | flops | bytes accessed | tf_op | source)
XLA Modules:
  0.0 109.4 jit_solution(7806863780088703125)
XLA Ops:
  0.6 104.0 %shard_map.103 = (bf16[32,448]{1,0:T(8,128)(2,1)}, bf16[304,448]{1,0:T(8,128)(2,1)}, bf16[304,448]{1,0:T(8,128)(2,1)}) custom-call(bf16[32,448]{1,0:T(8,128)(2,1)} %g_hbm.1, f32[2,32]{1,0:T(2,128)} %bitcast.12, s32[2,32]{1,0:T(2,128)} %bitcast.13, bf16[4,448,2048]{2,1,0:T(8,128)(2,1)} %bitcast.8, bf16[304,2048]{1,0:T(8,128)(2,1)} %bitcast.9, ...), custom_call_target="tpu_custom_call" | custom-call | flops 4000000000 | bytes 8000000 | tf_op jit(solution)/shard_map/pallas_call | solution.py:346
  104.6 1.4 %copy.14 = bf16[32,448]{1,0:T(8,128)(2,1)} copy(bf16[32,448]{1,0:T(8,128)(2,1)} %get-tuple-element.12) | data formatting | bytes 57344
  106.0 1.7 %copy.15 = bf16[448,304]{0,1:T(8,128)(2,1)} copy(bf16[448,304]{0,1:T(8,128)(2,1)} %bitcast.7) | data formatting | bytes 544768
  107.7 1.7 %copy.16 = bf16[304,448]{1,0:T(8,128)(2,1)} copy(bf16[304,448]{1,0:T(8,128)(2,1)} %get-tuple-element.14) | data formatting | bytes 544768

commit v3 on v2

--- a/solution.py
+++ b/solution.py
@@ -32,8 +32,8 @@
     g_hbm, probs_hbm, ids_hbm, x_hbm, gate_hbm, up_hbm, wup_hbm, wdown_hbm,
     tok_out, gup_out, gdown_out,
     g_ref, probs_ref, ids_ref, shard, gath, place, routed, routed2, wdown, wdown2, wup, gate, up, xt, pair, unit, terms,
-    tok, yrecv, drecv, reduced, final, down_sum,
-    ld_sem, s1, r1, s2, r2, ws, wr, cs, cr, ys, yr, us, ur, fs, fr, ds, dr, es, er,
+    tok, yrecv, drecv, reduced, final, total,
+    ld_sem, s1, r1, s0, r0, s2, r2, ws, wr, cs, cr, ys, yr, us, ur, fs, fr, ds, dr, es, er,
 ):
     pos, dpos = lax.axis_index("expert"), lax.axis_index("dp")
     z, x = pos // N, pos % N
@@ -76,7 +76,7 @@
         load.start()
 
     barrier = pltpu.get_barrier_semaphore()
-    partners = [on_x(d) for d in range(1, N)] + [on_z(d) for d in range(1, N)] + [on_y(1), on_y(-1), other]
+    partners = [on_x(d) for d in range(1, N)] + [on_z(d) for d in range(1, N)] + [on_y(d) for d in (1, -1, 2, -2)] + [other]
     for dev in partners:
         pl.semaphore_signal(barrier, inc=1, device_id=dev, device_id_type=MESH)
 
@@ -119,22 +119,37 @@
         return ref.at[h, index, pl.ds(2 * c, 2)]
 
     inflight = {}
-    for k in range(N // 2 + 1):
+    for j in (0, 1, 7, 2, 6, 3, 5, 4):
+        for h in range(2):
+            if j > 0:
+                first[h, j].wait_recv()
+            view = gath.at[h, here[h], j]
+            for r in range(2):
+                inflight[h, r, j] = remote(view, view, s0.at[j, h, r], r0.at[j, h, r], along[h](1 if r else -1))
+    for k in (1, 2, 3):
         for c in (0, 3, 1, 2):
             for h in range(2):
-                if k == 0:
-                    for j in (2 * c, 2 * c + 1):
-                        if j > 0:
-                            first[h, j].wait_recv()
                 for r in range(2):
                     sign, far = (1 if r else -1), hops(r, c)
-                    if 1 <= k <= far:
+                    if k == 1:
+                        inflight[h, r, 2 * c].wait_recv()
+                        inflight[h, r, 2 * c + 1].wait_recv()
+                    else:
                         inflight[k - 1, c, h, r].wait_recv()
-                    if k < far:
-                        view = piece(gath, h, (here[h] - sign * k + N) % N, c)
+                    view = piece(gath, h, (here[h] - sign * k + N) % N, c)
+                    if k == 2 and far == 4:
+                        inflight[3, c, h, r] = remote(
+                            view, view, s2.at[3, c, h, r], r2.at[3, c, h, r], along[h](2 * sign)
+                        )
+                    if k < 3:
                         inflight[k, c, h, r] = remote(
                             view, view, s2.at[k, c, h, r], r2.at[k, c, h, r], along[h](sign)
                         )
+    for c in range(PIECES):
+        for h in range(2):
+            for r in range(2):
+                if hops(r, c) == 4:
+                    inflight[3, c, h, r].wait_recv()
 
     lane_id = lax.broadcasted_iota(jnp.int32, (ROWS, ROWS), 1)
     row_id = lax.broadcasted_iota(jnp.int32, (ROWS, 1), 0)
@@ -175,55 +190,73 @@
     for g in range(GROUPS):
         swap(g).wait_recv()
 
-    def partial(i):
-        mine = routed[pl.ds(core * 16 + 2 * i, 2)].reshape(128, 448)
-        theirs = routed2[pl.ds(2 * i, 2)].reshape(128, 448)
-        dims = (((1,), (1,)), ((), ()))
-        pair[i] = (
-            lax.dot_general(wdown[...], mine, dims, preferred_element_type=F32)
-            + lax.dot_general(wdown2[...], theirs, dims, preferred_element_type=F32)
-        ).astype(BF16)
-
-    def down_block(b):
-        span = pl.ds(512 * b, 512)
-        hidden = (gate[:, span].astype(F32) * up[:, span].astype(F32)).astype(BF16)
-        rows = routed[8 * b:8 * b + 8].reshape(512, 448)
-        product = jnp.dot(hidden, rows, preferred_element_type=F32)
-        if b == 0:
-            down_sum[...] = product
-        elif b < 3:
-            down_sum[...] += product
-        else:
-            gdown_out[...] = (down_sum[...] + product).astype(BF16)
+    def partial(offset, count):
+        def step(n, carry):
+            i = (y + offset + N + n) % N
+            mine = routed[pl.ds(core * 16 + 2 * i, 2)].reshape(128, 448)
+            theirs = routed2[pl.ds(2 * i, 2)].reshape(128, 448)
+            dims = (((1,), (1,)), ((), ()))
+            pair[i] = (
+                lax.dot_general(wdown[...], mine, dims, preferred_element_type=F32)
+                + lax.dot_general(wdown2[...], theirs, dims, preferred_element_type=F32)
+            ).astype(BF16)
+            return carry
+
+        lax.fori_loop(0, count, step, 0)
+
+    def down_blocks(low):
+        def step(b, carry):
+            span = pl.ds(pl.multiple_of(512 * b, 512), 512)
+            hidden = (gate[:, span].astype(F32) * up[:, span].astype(F32)).astype(BF16)
+            rows = routed[pl.ds(8 * b, 8)].reshape(512, 448)
+            total[...] += jnp.dot(hidden, rows, preferred_element_type=F32)
+            return carry
+
+        lax.fori_loop(low, low + 2, step, 0)
+
+    def ring_start(far, sign, view, recv, ssem, rsem, dev):
+        copies = {}
+        if far == 4:
+            copies[0] = remote(view(4 * sign), recv(0), ssem(0), rsem(0), dev(2 * sign))
+        copies[far - 3] = remote(view(3 * sign), recv(far - 3), ssem(far - 3), rsem(far - 3), dev(sign))
+        return copies
+
+    def ring_step(stage, copies, far, sign, view, recv, ssem, rsem, dev):
+        own = view((3 - stage) * sign)
+        value = own[...].astype(F32)
+        for i in (0, 1) if (far, stage) == (4, 1) else (far + stage - 4,):
+            copies[i].wait_recv()
+            value = value + recv(i)[...].astype(F32)
+        own[...] = value.astype(BF16)
+        n = far + stage - 3
+        copies[n] = remote(own, recv(n), ssem(n), rsem(n), dev(sign))
+
+    def y_ring(c, r):
+        low, size = SPLIT[c]
+        return (
+            hops(r, c),
+            1 if r else -1,
+            lambda offset: pair.at[(y + offset + N) % N, pl.ds(low, size)],
+            lambda i: yrecv.at[i, c, r, pl.ds(0, size)],
+            lambda i: ys.at[i, c, r],
+            lambda i: yr.at[i, c, r],
+            on_y,
+        )
 
     inflight = {}
-    for far in (4, 3):
-        for offset in ((4,) if far == 4 else (3, -3)):
-            partial((y + offset + N) % N)
-        for c, (low, size) in enumerate(SPLIT):
-            for r in range(2):
-                if hops(r, c) == far:
-                    view = pair.at[(y + (far if r else -far) + N) % N, pl.ds(low, size)]
-                    inflight[0, c, r] = remote(
-                        view, yrecv.at[0, c, r, pl.ds(0, size)], ys.at[0, c, r], yr.at[0, c, r], on_y(1 if r else -1)
-                    )
-    for offset in (2, -2, 1, -1, 0):
-        partial((y + offset + N) % N)
-    for k in range(1, N // 2):
-        for c, (low, size) in enumerate(SPLIT):
-            for r in range(2):
-                sign, far = (1 if r else -1), hops(r, c)
-                if k < far:
-                    view = pair.at[(y + sign * (far - k) + N) % N, pl.ds(low, size)]
-                    inflight[k - 1, c, r].wait_recv()
-                    view[...] = add(view[...], yrecv[k - 1, c, r, 0:size]).astype(BF16)
-                    inflight[k, c, r] = remote(
-                        view, yrecv.at[k, c, r, pl.ds(0, size)], ys.at[k, c, r], yr.at[k, c, r], on_y(sign)
-                    )
-        if k == 1:
-            for load in loads[4:6]:
-                load.wait()
-        down_block(k - 1)
+    partial(3, 3)
+    for c in range(PIECES):
+        for r in range(2):
+            inflight[c, r] = ring_start(*y_ring(c, r))
+    partial(-2, 5)
+    total[...] = jnp.zeros_like(total)
+    for load in loads[4:6]:
+        load.wait()
+    for stage in (1, 2):
+        for c in range(PIECES):
+            for r in range(2):
+                ring_step(stage, inflight[c, r], *y_ring(c, r))
+        down_blocks(2 * stage - 2)
     for load in loads[6:]:
         load.wait()
 
@@ -231,11 +264,11 @@
     lanes = pl.ds(pl.multiple_of(mine * 128, 128), 128)
     gathering = {}
     for c, (low, size) in enumerate(SPLIT):
-        total = pair[y, low:low + size].astype(F32)
+        whole = pair[y, low:low + size].astype(F32)
         for r in range(2):
-            inflight[hops(r, c) - 1, c, r].wait_recv()
-            total = total + yrecv[hops(r, c) - 1, c, r, 0:size].astype(F32)
-        unit[mine, low:low + size] = (total * gate[low:low + size, lanes].astype(F32)).astype(BF16)
+            inflight[c, r][hops(r, c) - 1].wait_recv()
+            whole = whole + yrecv[hops(r, c) - 1, c, r, 0:size].astype(F32)
+        unit[mine, low:low + size] = (whole * gate[low:low + size, lanes].astype(F32)).astype(BF16)
         view = unit.at[mine, pl.ds(low, size)]
         for r in range(2):
             gathering[0, c, r] = remote(view, view, us.at[0, c, r], ur.at[0, c, r], on_y(1 if r else -1))
@@ -245,41 +278,55 @@
         view = unit.at[core * N + index, pl.ds(HALVES[h][0], HALVES[h][1])]
         across[k, h, r] = remote(view, view, fs.at[k, h, r], fr.at[k, h, r], other)
 
-    def slot_block(b):
-        rows = lax.dot_general(unit[b], wup[...], (((0,), (0,)), ((), ())), preferred_element_type=F32)
-        terms[pl.ds(2 * b, 2)] = rows.astype(BF16).reshape(2, 64, 448)
+    def slot_blocks(owner, offset, stride, count):
+        def step(n, carry):
+            b = owner * N + (y + offset + N + stride * n) % N
+            rows = lax.dot_general(unit[b], wup[...], (((0,), (0,)), ((), ())), preferred_element_type=F32)
+            terms[pl.ds(2 * b, 2)] = rows.astype(BF16).reshape(2, 64, 448)
+            return carry
+
+        lax.fori_loop(0, count, step, 0)
+
+    def arrived(k):
+        for h in range(2):
+            for r in range(2):
+                if (k, h, r) in across:
+                    across[k, h, r].wait_recv()
 
     for h in range(2):
         cross_half(0, h, 1, y)
-    down_block(3)
-    slot_block(mine)
-
-    def theirs(k):
-        for h in range(2):
-            for r in range(2):
-                if (k, h, r) in across:
-                    across[k, h, r].wait_recv()
-        slot_block((1 - core) * N + (y + k) % N)
-        if 0 < k < N // 2:
-            slot_block((1 - core) * N + (y - k + N) % N)
-
-    for k in range(1, N // 2 + 1):
+    gdown_out[...] = total[...].astype(BF16)
+    slot_blocks(core, 0, 1, 1)
+    for k in (1, 2, 3):
         for c, (low, size) in enumerate(SPLIT):
             for r in range(2):
                 sign, far = (1 if r else -1), hops(r, c)
                 index = (y - sign * k + N) % N
-                if k <= far:
-                    gathering[k - 1, c, r].wait_recv()
-                if k < far:
-                    view = unit.at[core * N + index, pl.ds(low, size)]
+                gathering[k - 1, c, r].wait_recv()
+                view = unit.at[core * N + index, pl.ds(low, size)]
+                if k == 2 and far == 4:
+                    gathering[3, c, r] = remote(view, view, us.at[3, c, r], ur.at[3, c, r], on_y(2 * sign))
+                if k < 3:
                     gathering[k, c, r] = remote(view, view, us.at[k, c, r], ur.at[k, c, r], on_y(sign))
-                if k <= far and c % 2 == 1:
+                if c % 2 == 1:
                     cross_half(k, c // 2, r, index)
-        slot_block(core * N + (y + k) % N)
-        if k < N // 2:
-            slot_block(core * N + (y - k + N) % N)
-        theirs(k - 1)
-    theirs(N // 2)
+        if k < 3:
+            slot_blocks(core, -k, 2 * k, 2)
+            arrived(k - 1)
+            slot_blocks(1 - core, 1 - k, 2 * k - 2, min(k, 2))
+    for c in range(PIECES):
+        for r in range(2):
+            if hops(r, c) == 4:
+                gathering[3, c, r].wait_recv()
+                if c % 2 == 1:
+                    cross_half(4, c // 2, r, (y + 4) % N)
+    slot_blocks(core, 3, 1, 3)
+    arrived(2)
+    slot_blocks(1 - core, -2, 4, 2)
+    arrived(3)
+    arrived(4)
+    slot_blocks(1 - core, 3, 1, 3)
+    total[...] = jnp.zeros_like(total)
 
     def to_tokens(g, carry):
         start = pl.multiple_of(16 * g, 16)
@@ -292,35 +339,47 @@
 
     lax.fori_loop(0, GROUPS, to_tokens, 0)
 
+    def token_ring(c, h, r):
+        return (
+            hops(r, c),
+            1 if r else -1,
+            lambda offset: piece(tok, h, (here[h] + offset + N) % N, c),
+            lambda i: drecv.at[i, c, h, r],
+            lambda i: ds.at[i, c, h, r],
+            lambda i: dr.at[i, c, h, r],
+            along[h],
+        )
+
+    def up_blocks(low, count):
+        def step(b, carry):
+            span = pl.ds(pl.multiple_of(b * 128, 128), 128)
+            total[...] += lax.dot_general(
+                unit[b], xt[:, span], (((1,), (1,)), ((), ())), preferred_element_type=F32
+            )
+            return carry
+
+        lax.fori_loop(low, low + count, step, 0)
+
     inflight = {}
-    for k in range(N // 2):
+    for stage in range(3):
         for c in range(PIECES):
             for h in range(2):
                 for r in range(2):
-                    sign, far = (1 if r else -1), hops(r, c)
-                    view = piece(tok, h, (here[h] + sign * (far - k) + N) % N, c)
-                    if 1 <= k < far:
-                        inflight[k - 1, c, h, r].wait_recv()
-                        view[...] = add(view[...], drecv[k - 1, c, h, r]).astype(BF16)
-                    if k < far:
-                        inflight[k, c, h, r] = remote(
-                            view, drecv.at[k, c, h, r], ds.at[k, c, h, r], dr.at[k, c, h, r], along[h](sign)
-                        )
-
-    def up_block(b, carry):
-        span = pl.ds(pl.multiple_of(b * 128, 128), 128)
-        return carry + lax.dot_general(unit[b], xt[:, span], (((1,), (1,)), ((), ())), preferred_element_type=F32)
-
-    gup_out[...] = lax.fori_loop(0, 2 * N, up_block, jnp.zeros((304, 448), F32)).astype(BF16)
+                    if stage == 0:
+                        inflight[c, h, r] = ring_start(*token_ring(c, h, r))
+                    else:
+                        ring_step(stage, inflight[c, h, r], *token_ring(c, h, r))
+        up_blocks((0, 6, 11)[stage], (6, 5, 5)[stage])
+    gup_out[...] = total[...].astype(BF16)
 
     last = []
     for c in range(PIECES):
         for h in range(2):
-            total = piece(tok, h, here[h], c)[...].astype(F32)
-            for r in range(2):
-                inflight[hops(r, c) - 1, c, h, r].wait_recv()
-                total = total + drecv[hops(r, c) - 1, c, h, r].astype(F32)
-            reduced[h, 2 * c:2 * c + 2] = total.astype(BF16)
+            whole = piece(tok, h, here[h], c)[...].astype(F32)
+            for r in range(2):
+                inflight[c, h, r][hops(r, c) - 1].wait_recv()
+                whole = whole + drecv[hops(r, c) - 1, c, h, r].astype(F32)
+            reduced[h, 2 * c:2 * c + 2] = whole.astype(BF16)
             for d in (2 * c, 2 * c + 1):
                 if d > 0:
                     last.append(
@@ -329,10 +388,10 @@
     for copy in last:
         copy.wait_recv()
     for h in range(2):
-        total = reduced[h, 0].astype(F32)
+        whole = reduced[h, 0].astype(F32)
         for d in range(1, N):
-            total = total + final[h, d - 1].astype(F32)
-        tok_out[16 * h:16 * h + 16, :] = total.astype(BF16)
+            whole = whole + final[h, d - 1].astype(F32)
+        tok_out[16 * h:16 * h + 16, :] = whole.astype(BF16)
     for copy in sent:
         copy.wait_send()
     for g in range(GROUPS):
@@ -378,6 +437,7 @@
             pltpu.VMEM((units, width), F32),
             dma((8,)),
             dma((2, N - 1)), dma((2, N - 1)),
+            dma((N, 2, 2)), dma((N, 2, 2)),
             dma((4, PIECES, 2, 2)), dma((4, PIECES, 2, 2)),
             dma((1,)), dma((1,)),
             dma((GROUPS,)), dma((GROUPS,)),

time: 110 us -> 102 us (0.927)
  the two profiles are of different devices: /device:TPU:16 before, /device:TPU:2 now
where the time goes in v3:
time: 102 us; the launch traced here: 101 us
  Pallas kernels  96 us (94%)
  local copies, waits for them, and re-layouts  4.79 us (5%)
    pallas_call x1, Pallas kernels, body(): pl.pallas_call(kernel, out_shape=(jax.ShapeDtypeStruct((TOK, width), BF16...  96 us
    unnamed x3, local copies, waits for them, and re-layouts  4.79 us

profile of v3, /device:TPU:2, one launch (start us, length us, event | category | flops | bytes accessed | tf_op | source)
XLA Modules:
  0.0 101.4 jit_solution(8328344719687680026)
XLA Ops:
  0.6 96.0 %shard_map.103 = (bf16[32,448]{1,0:T(8,128)(2,1)}, bf16[304,448]{1,0:T(8,128)(2,1)}, bf16[304,448]{1,0:T(8,128)(2,1)}) custom-call(bf16[32,448]{1,0:T(8,128)(2,1)} %g_hbm.1, f32[2,32]{1,0:T(2,128)} %bitcast.12, s32[2,32]{1,0:T(2,128)} %bitcast.13, bf16[4,448,2048]{2,1,0:T(8,128)(2,1)} %bitcast.8, bf16[304,2048]{1,0:T(8,128)(2,1)} %bitcast.9, ...), custom_call_target="tpu_custom_call" | custom-call | flops 4000000000 | bytes 8000000 | tf_op jit(solution)/shard_map/pallas_call | solution.py:405
  96.6 1.4 %copy.14 = bf16[32,448]{1,0:T(8,128)(2,1)} copy(bf16[32,448]{1,0:T(8,128)(2,1)} %get-tuple-element.12) | data formatting | bytes 57344
  98.0 1.7 %copy.15 = bf16[448,304]{0,1:T(8,128)(2,1)} copy(bf16[448,304]{0,1:T(8,128)(2,1)} %bitcast.7) | data formatting | bytes 544768
  99.7 1.7 %copy.16 = bf16[304,448]{1,0:T(8,128)(2,1)} copy(bf16[304,448]{1,0:T(8,128)(2,1)} %get-tuple-element.14) | data formatting | bytes 544768

commit v4 on v3

--- a/solution.py
+++ b/solution.py
@@ -31,7 +31,7 @@
 def kernel(
     g_hbm, probs_hbm, ids_hbm, x_hbm, gate_hbm, up_hbm, wup_hbm, wdown_hbm,
     tok_out, gup_out, gdown_out,
-    g_ref, probs_ref, ids_ref, shard, gath, place, routed, routed2, wdown, wdown2, wup, gate, up, xt, pair, unit, terms,
+    g_ref, probs_ref, ids_ref, shard, gath, place, scaled, routed, routed2, wdown, wdown2, wup, gate, up, xt, pair, unit, terms,
     tok, yrecv, drecv, reduced, final, total,
     ld_sem, s1, r1, s0, r0, s2, r2, ws, wr, cs, cr, ys, yr, us, ur, fs, fr, ds, dr, es, er,
 ):
@@ -88,22 +88,26 @@
     shard[:, 384:512] = jnp.zeros((TOK, 128), BF16)
     shard[:, 0:448] = g_ref[...]
     tail = shard[:, 384:512].astype(F32)
-    for e in range(EXPERTS):
-        named = ids_ref[...] == e
-        prob_row = jnp.sum(jnp.where(named, probs_ref[...], 0.0), axis=0, keepdims=True)
-        used_row = jnp.sum(jnp.where(named, 1.0, 0.0), axis=0, keepdims=True)
-        prob = jnp.sum(jnp.where(lane32 == row32, prob_row, 0.0), axis=1, keepdims=True)
-        used = jnp.sum(jnp.where(lane32 == row32, used_row, 0.0), axis=1, keepdims=True)
-        before = jnp.sum(jnp.where(lane32 < row32, used_row, 0.0), axis=1, keepdims=True)
-        high = prob.astype(BF16).astype(F32)
-        middle = (prob - high).astype(BF16).astype(F32)
-        rank = used * (before + 1.0) - 1.0
-        for i, column in enumerate((high, middle, prob - high - middle, rank)):
-            tail = jnp.where(lane128 == 64 + 4 * e + i, column, tail)
+    def column(row):
+        return jnp.sum(jnp.where(lane32 == row32, row, 0.0), axis=1, keepdims=True)
+
+    ids = ids_ref[...].astype(F32)
+    expert_of_lane = ((lane128 - 64) // 4).astype(F32)
+    ones = column(ids[0:1]) == expert_of_lane
+    twos = column(ids[1:2]) == expert_of_lane
+    prob = jnp.where(ones, column(probs_ref[0:1]), 0.0) + jnp.where(twos, column(probs_ref[1:2]), 0.0)
+    used = jnp.where(ones, 1.0, 0.0) + jnp.where(twos, 1.0, 0.0)
+    lower = jnp.where(lane32 < row32, 1.0, 0.0).astype(BF16)
+    before = jnp.dot(lower, used.astype(BF16), preferred_element_type=F32)
+    high = prob.astype(BF16).astype(F32)
+    middle = (prob - high).astype(BF16).astype(F32)
+    kind = lane128 % 4
+    extra = jnp.where(kind == 0, high, jnp.where(kind == 1, middle, prob - high - middle))
+    extra = jnp.where(kind == 3, used * (before + 1.0) - 1.0, extra)
+    tail = jnp.where(lane128 >= 64, extra, tail)
     shard[:, 384:512] = tail.astype(BF16)
     for h in range(2):
         gath[h, here[h], 0] = shard[16 * h:16 * h + 16, :]
-    loads[3].wait()
 
     pl.semaphore_wait(barrier, len(partners))
 
@@ -113,6 +117,7 @@
             first[h, N - d] = remote(
                 gath.at[h, here[h], 0], gath.at[h, here[h], N - d], s1.at[h, d - 1], r1.at[h, N - d - 1], along[1 - h](d)
             )
+    loads[3].wait()
     down_swap = remote(wdown, wdown2, ws.at[0], wr.at[0], other)
 
     def piece(ref, h, index, c):
@@ -126,7 +131,7 @@
             view = gath.at[h, here[h], j]
             for r in range(2):
                 inflight[h, r, j] = remote(view, view, s0.at[j, h, r], r0.at[j, h, r], along[h](1 if r else -1))
-    for k in (1, 2, 3):
+    for k in (1, 2):
         for c in (0, 3, 1, 2):
             for h in range(2):
                 for r in range(2):
@@ -141,23 +146,51 @@
                         inflight[3, c, h, r] = remote(
                             view, view, s2.at[3, c, h, r], r2.at[3, c, h, r], along[h](2 * sign)
                         )
-                    if k < 3:
-                        inflight[k, c, h, r] = remote(
-                            view, view, s2.at[k, c, h, r], r2.at[k, c, h, r], along[h](sign)
-                        )
+                    inflight[k, c, h, r] = remote(
+                        view, view, s2.at[k, c, h, r], r2.at[k, c, h, r], along[h](sign)
+                    )
+
+    lane_id = lax.broadcasted_iota(jnp.int32, (128, ROWS), 1)
+    step_id = lax.broadcasted_iota(jnp.int32, (128, 1), 0) // 16
+    tail_lane = lax.broadcasted_iota(jnp.int32, (128, 128), 1) - 64 - 4 * expert
+
+    def onehot_and_scaled(rows, source):
+        extra = rows[:, 384:512].astype(F32)
+        weight = jnp.sum(jnp.where((tail_lane >= 0) & (tail_lane < 3), extra, 0.0), axis=1, keepdims=True)
+        rank = jnp.sum(jnp.where(tail_lane == 3, extra, 0.0), axis=1, keepdims=True)
+        key = rank.astype(jnp.int32) * 16 + source
+        return jnp.where(key == lane_id, 1.0, 0.0).astype(BF16), (rows.astype(F32) * weight).astype(BF16)
+
+    def planes(offset, stride, count):
+        def step(n, carry):
+            zz = (z + offset + N + stride * n) % N
+            xx = (x + offset + N + stride * n) % N
+            low = pl.ds(pl.multiple_of((zz % 2) * 128, 128), 128)
+            onehot, rows = onehot_and_scaled(
+                gath[0, zz].reshape(128, 512), (zz % 2) * 8 + (x + step_id) % 8
+            )
+            place[zz // 2, low] = onehot
+            scaled[zz // 2, low] = rows
+            onehot, rows = onehot_and_scaled(
+                gath[1, xx].reshape(128, 512), ((z + step_id) % 2) * 8 + xx
+            )
+            for j in range(N):
+                zj = (z + j) % N
+                at = pl.ds(pl.multiple_of(256 + (zj % 2) * 128 + xx * 16, 16), 16)
+                place[zj // 2, at] = onehot[16 * j:16 * j + 16]
+                scaled[zj // 2, at] = rows[16 * j:16 * j + 16]
+            return carry
+
+        lax.fori_loop(0, count, step, 0)
+
+    planes(-2, 1, 5)
     for c in range(PIECES):
         for h in range(2):
             for r in range(2):
+                inflight[2, c, h, r].wait_recv()
                 if hops(r, c) == 4:
                     inflight[3, c, h, r].wait_recv()
-
-    lane_id = lax.broadcasted_iota(jnp.int32, (ROWS, ROWS), 1)
-    row_id = lax.broadcasted_iota(jnp.int32, (ROWS, 1), 0)
-    tile = (row_id % 256) // 16
-    source = jnp.where(
-        row_id < 256, (tile // 8) * 8 + (tile % 8 + x) % 8, (tile // 8) * 8 + tile % 8
-    )
-    tail_lane = lax.broadcasted_iota(jnp.int32, (ROWS, 128), 1) - 64 - 4 * expert
+    planes(3, 1, 3)
 
     def swap(g):
         span = pl.ds(pl.multiple_of(16 * g, 16), 16)
@@ -167,18 +200,7 @@
         )
 
     def to_slots(g, carry):
-        one = gath[0, pl.ds(2 * g, 2)].reshape(256, 512)
-        two = gath[1, :, (2 * g - z + N) % N].reshape(128, 512)
-        three = gath[1, :, (2 * g + 1 - z + N) % N].reshape(128, 512)
-        rows = jnp.concatenate([one, two, three], axis=0)
-        extra = rows[:, 384:512].astype(F32)
-        weight = jnp.sum(jnp.where((tail_lane >= 0) & (tail_lane < 3), extra, 0.0), axis=1, keepdims=True)
-        rank = jnp.sum(jnp.where(tail_lane == 3, extra, 0.0), axis=1, keepdims=True)
-        key = rank.astype(jnp.int32) * 16 + source
-        onehot = jnp.where(key == lane_id, 1.0, 0.0).astype(BF16)
-        place[g] = onehot
-        scaled = (rows.astype(F32) * weight).astype(BF16)
-        moved = lax.dot_general(onehot, scaled, (((0,), (0,)), ((), ())), preferred_element_type=F32)
+        moved = lax.dot_general(place[g], scaled[g], (((0,), (0,)), ((), ())), preferred_element_type=F32)
         start = pl.multiple_of(16 * g, 16)
         routed[:, pl.ds(start, 16), :] = moved[:, 0:448].astype(BF16).reshape(CAP, 16, 448)
         swap(g).start()
@@ -418,6 +440,7 @@
             pltpu.VMEM((TOK, 512), BF16),
             pltpu.VMEM((2, N, N, 16, 512), BF16),
             pltpu.VMEM((GROUPS, ROWS, ROWS), BF16),
+            pltpu.VMEM((GROUPS, ROWS, 512), BF16),
             pltpu.VMEM((CAP, N * N, width), BF16),
             pltpu.VMEM((CAP // 2, N * N, width), BF16),
             pltpu.VMEM((units, width), BF16),

time: 102 us -> 102 us (level)
  the two profiles are of different devices: /device:TPU:2 before, /device:TPU:16 now
where the time goes in v4:
time: 102 us; the launch traced here: 101 us
  Pallas kernels  95.8 us (94%)
  local copies, waits for them, and re-layouts  4.79 us (5%)
    pallas_call x1, Pallas kernels, body(): pl.pallas_call(kernel, out_shape=(jax.ShapeDtypeStruct((TOK, width), BF16...  95.8 us
    unnamed x3, local copies, waits for them, and re-layouts  4.79 us

profile of v4, /device:TPU:16, one launch (start us, length us, event | category | flops | bytes accessed | tf_op | source)
XLA Modules:
  0.0 101.2 jit_solution(7569739332266281717)
XLA Ops:
  0.6 95.8 %shard_map.103 = (bf16[32,448]{1,0:T(8,128)(2,1)}, bf16[304,448]{1,0:T(8,128)(2,1)}, bf16[304,448]{1,0:T(8,128)(2,1)}) custom-call(bf16[32,448]{1,0:T(8,128)(2,1)} %g_hbm.1, f32[2,32]{1,0:T(2,128)} %bitcast.12, s32[2,32]{1,0:T(2,128)} %bitcast.13, bf16[4,448,2048]{2,1,0:T(8,128)(2,1)} %bitcast.8, bf16[304,2048]{1,0:T(8,128)(2,1)} %bitcast.9, ...), custom_call_target="tpu_custom_call" | custom-call | flops 4000000000 | bytes 8000000 | tf_op jit(solution)/shard_map/pallas_call | solution.py:427
  96.5 1.4 %copy.14 = bf16[32,448]{1,0:T(8,128)(2,1)} copy(bf16[32,448]{1,0:T(8,128)(2,1)} %get-tuple-element.12) | data formatting | bytes 57344
  97.8 1.7 %copy.15 = bf16[448,304]{0,1:T(8,128)(2,1)} copy(bf16[448,304]{0,1:T(8,128)(2,1)} %bitcast.7) | data formatting | bytes 544768
  99.5 1.7 %copy.16 = bf16[304,448]{1,0:T(8,128)(2,1)} copy(bf16[304,448]{1,0:T(8,128)(2,1)} %get-tuple-element.14) | data formatting | bytes 544768

commit v5 on v4

--- a/solution.py
+++ b/solution.py
@@ -320,6 +320,9 @@
     gdown_out[...] = total[...].astype(BF16)
     slot_blocks(core, 0, 1, 1)
     for k in (1, 2, 3):
+        if k == 3:
+            arrived(2)
+            slot_blocks(1 - core, -2, 4, 2)
         for c, (low, size) in enumerate(SPLIT):
             for r in range(2):
                 sign, far = (1 if r else -1), hops(r, c)
@@ -343,14 +346,13 @@
                 if c % 2 == 1:
                     cross_half(4, c // 2, r, (y + 4) % N)
     slot_blocks(core, 3, 1, 3)
-    arrived(2)
-    slot_blocks(1 - core, -2, 4, 2)
     arrived(3)
     arrived(4)
     slot_blocks(1 - core, 3, 1, 3)
     total[...] = jnp.zeros_like(total)
 
-    def to_tokens(g, carry):
+    def to_tokens(n, carry):
+        g = (z // 2 + 1 + n) % GROUPS
         start = pl.multiple_of(16 * g, 16)
         rows = terms[:, pl.ds(start, 16), :].reshape(ROWS, 448)
         back = jnp.dot(place[g], rows, preferred_element_type=F32).astype(BF16)
@@ -358,8 +360,6 @@
         tok[1, :, (2 * g - z + N) % N] = back[256:384].reshape(N, 16, 448)
         tok[1, :, (2 * g + 1 - z + N) % N] = back[384:512].reshape(N, 16, 448)
         return carry
-
-    lax.fori_loop(0, GROUPS, to_tokens, 0)
 
     def token_ring(c, h, r):
         return (
@@ -383,13 +383,19 @@
         lax.fori_loop(low, low + count, step, 0)
 
     inflight = {}
+    lax.fori_loop(0, GROUPS - 1, to_tokens, 0)
     for stage in range(3):
-        for c in range(PIECES):
+        if stage == 0:
             for h in range(2):
-                for r in range(2):
-                    if stage == 0:
+                for c in range(PIECES):
+                    for r in range(2):
                         inflight[c, h, r] = ring_start(*token_ring(c, h, r))
-                    else:
+                if h == 0:
+                    lax.fori_loop(GROUPS - 1, GROUPS, to_tokens, 0)
+        else:
+            for c in range(PIECES):
+                for h in range(2):
+                    for r in range(2):
                         ring_step(stage, inflight[c, h, r], *token_ring(c, h, r))
         up_blocks((0, 6, 11)[stage], (6, 5, 5)[stage])
     gup_out[...] = total[...].astype(BF16)

time: 102 us -> 101 us (level)
  the two profiles are of different devices: /device:TPU:16 before, /device:TPU:2 now
where the time goes in v5:
time: 101 us
  Pallas kernels  95.3 us (94%)
  local copies, waits for them, and re-layouts  4.79 us (5%)
    pallas_call x1, Pallas kernels, body(): pl.pallas_call(kernel, out_shape=(jax.ShapeDtypeStruct((TOK, width), BF16...  95.3 us
    unnamed x3, local copies, waits for them, and re-layouts  4.79 us

profile of v5, /device:TPU:2, one launch (start us, length us, event | category | flops | bytes accessed | tf_op | source)
XLA Modules:
  0.0 100.7 jit_solution(3305089882246835098)
XLA Ops:
  0.6 95.3 %shard_map.103 = (bf16[32,448]{1,0:T(8,128)(2,1)}, bf16[304,448]{1,0:T(8,128)(2,1)}, bf16[304,448]{1,0:T(8,128)(2,1)}) custom-call(bf16[32,448]{1,0:T(8,128)(2,1)} %g_hbm.1, f32[2,32]{1,0:T(2,128)} %bitcast.12, s32[2,32]{1,0:T(2,128)} %bitcast.13, bf16[4,448,2048]{2,1,0:T(8,128)(2,1)} %bitcast.8, bf16[304,2048]{1,0:T(8,128)(2,1)} %bitcast.9, ...), custom_call_target="tpu_custom_call" | custom-call | flops 4000000000 | bytes 8000000 | tf_op jit(solution)/shard_map/pallas_call | solution.py:433
  95.9 1.4 %copy.14 = bf16[32,448]{1,0:T(8,128)(2,1)} copy(bf16[32,448]{1,0:T(8,128)(2,1)} %get-tuple-element.12) | data formatting | bytes 57344
  97.3 1.7 %copy.15 = bf16[448,304]{0,1:T(8,128)(2,1)} copy(bf16[448,304]{0,1:T(8,128)(2,1)} %bitcast.7) | data formatting | bytes 544768
  99.0 1.7 %copy.16 = bf16[304,448]{1,0:T(8,128)(2,1)} copy(bf16[304,448]{1,0:T(8,128)(2,1)} %get-tuple-element.14) | data formatting | bytes 544768
